TPU v7x, 256 devices: a whole 4x4x8 slice. The times are simulated.
256 devices in a mesh: tm: 8 (over y, z_lo), col: 32 (over x, z_hi, core).
Axes of the slice: x: 4, y: 4, z: 8 (z_hi: 4, z_lo: 2; z = z_hi * 2 + z_lo), core: 2. Of those that a mesh axis runs over, the one named last changes fastest.
Arguments:
- visibilities: float32 [64, 32, 2, 2048], P('tm', 'col'), may hold values from -6 to 6
- coords: float32 [64, 32, 2, 2048], P('tm', 'col'), may hold values from 3 to 124
- tile_row: int32 [64, 32], P('tm', 'col'), may hold values from 0 to 15
- counts: int32 [8, 32], P('tm', 'col'), may hold values from 1 to 8, as said below
- w_plane: float32 [1], replicated, may hold values from 20 to 60
Outputs:
- image_real: float32 [2048, 4096], P('tm', 'col')
- image_imag: float32 [2048, 4096], P('tm', 'col')
Inputs may be any that keep to these rules, and one draw needn't show every extreme that they name: `counts`: slots of a device from its count on carry no used blocks; in every draw one device uses all 8 slots.
All inputs are finite; a program needn't handle non-finite values.
Results may differ from a plain program's by a relative error of at most 0.01.
Values sent between devices are 32-bit elements; how exact they have to be, the bound alone decides.
No kernel may reach another device: no remote copies, remote signals or barrier semaphores. Data moves between devices by JAX's collectives and lax.ppermute only.
A program may use at most 320 MiB of HBM per device.

v0:
```python
import math

import jax
import jax.numpy as jnp
from jax import lax
from jax.sharding import PartitionSpec as P

TILE = 128
TROWS = 16


kernel_radius = 1.0
highest = lax.Precision.HIGHEST
pair_size = 2


def taper(position, cells):
    offset = cells[None, None, :] - position[:, :, None]
    inside = 1.0 - offset * offset / (kernel_radius * kernel_radius)
    inside = jnp.maximum(inside, 0.0)
    return inside * inside


def trig_table(first, second, length):
    product = first[:, None] * second[None, :] % length
    angle = product.astype(jnp.float32) * (2.0 * math.pi / length)
    return (jnp.cos(angle), jnp.sin(angle))


def matmul(left, right):
    return jnp.dot(left, right, precision=highest, preferred_element_type=jnp.float32)


def w_correct(real_image, imaginary_image, x_index, y_index, plane_depth, size_u, size_v):
    along_l = (x_index - size_u // 2).astype(jnp.float32) / size_u
    along_m = (y_index - size_v // 2).astype(jnp.float32) / size_v
    height = jnp.sqrt(
        1.0 - along_l[:, None] * along_l[:, None] - along_m[None, :] * along_m[None, :]
    )
    phase = 2.0 * math.pi * plane_depth * (height - 1.0)
    cosine = jnp.cos(phase)
    sine_part = jnp.sin(phase)
    scale = 1.0 / math.sqrt(size_u * size_v)
    real_out = (real_image * cosine - imaginary_image * sine_part) * scale
    imaginary_out = (real_image * sine_part + imaginary_image * cosine) * scale
    return (real_out, imaginary_out)


def grid_blocks(values, places, tile_rows, live_count):
    block_rows = values.shape[2]
    grid_rows = TILE * TROWS
    cells = jnp.arange(TILE, dtype=jnp.int32).astype(jnp.float32)
    anchor = jnp.zeros((), jnp.int32)

    def one_turn(turn_index, grid):
        first_slot = (turn_index * pair_size).astype(jnp.int32)
        value_pair = lax.dynamic_slice_in_dim(values, first_slot, pair_size, 0)
        place_pair = lax.dynamic_slice_in_dim(places, first_slot, pair_size, 0)
        row_pair = lax.dynamic_slice_in_dim(tile_rows, first_slot, pair_size, 0)
        living = first_slot + jnp.arange(pair_size, dtype=jnp.int32) < live_count
        weight_u = taper(place_pair[:, 0, :], cells).astype(jnp.bfloat16)
        weight_v = taper(place_pair[:, 1, :], cells).astype(jnp.bfloat16)
        weighted = jnp.swapaxes(value_pair, 1, 2)[:, :, :, None] * weight_u[:, :, None, :].astype(
            jnp.float32
        )
        weighted = jnp.where(living[:, None, None, None], weighted, 0.0).astype(jnp.bfloat16)
        weighted = weighted.reshape(pair_size, block_rows, 2 * TILE)
        partial_tiles = jnp.einsum(
            "gkj,gkq->gjq", weight_v, weighted, preferred_element_type=jnp.float32
        )
        partial_tiles = partial_tiles.reshape(pair_size, TILE, 2, TILE)
        for member in range(pair_size):
            corner = row_pair[member] * TILE
            current = lax.dynamic_slice(grid, (anchor, anchor, corner), (TILE, 2, TILE))
            grid = lax.dynamic_update_slice(
                grid, current + partial_tiles[member], (anchor, anchor, corner)
            )
        return grid

    turns = (live_count + pair_size - 1) // pair_size
    return lax.fori_loop(0, turns, one_turn, jnp.zeros((TILE, 2, grid_rows), jnp.float32))


def shards(visibilities, coords, tile_row, counts, w_plane):
    column_devices = lax.axis_size("col")
    slots = visibilities.shape[0]
    block_rows = visibilities.shape[3]
    values = visibilities.reshape(slots, 2, block_rows)
    places = coords.reshape(slots, 2, block_rows)
    tile_rows = tile_row.reshape(slots)
    live_count = counts.reshape(())
    grid = grid_blocks(values, places, tile_rows, live_count)
    local_grid = lax.psum_scatter(grid, "tm", scatter_dimension=2, tiled=True)
    local_rows = local_grid.shape[2]
    grid_rows = TILE * TROWS
    grid_columns = TILE * column_devices
    my_column = lax.axis_index("col")
    my_group = lax.axis_index("tm")
    y_block = min(512, grid_columns)
    per_column = local_rows // column_devices
    split_grid = local_grid.reshape(TILE, 2, column_devices, per_column)
    gathered = lax.all_to_all(split_grid, "col", split_axis=2, concat_axis=0, tiled=True)
    items = gathered.shape[3]
    real_part = (
        gathered[:, 0, 0, :]
        .reshape(column_devices, TILE, items)
        .transpose(1, 0, 2)
        .reshape(TILE, column_devices * items)
    )
    imaginary_part = (
        gathered[:, 1, 0, :]
        .reshape(column_devices, TILE, items)
        .transpose(1, 0, 2)
        .reshape(TILE, column_devices * items)
    )
    stacked_parts = jnp.concatenate(
        [
            jnp.concatenate([real_part, imaginary_part], 1),
            jnp.concatenate([-imaginary_part, real_part], 1),
        ],
        0,
    )
    inner_cells = jnp.arange(TILE, dtype=jnp.int32)
    outer_cells = jnp.arange(column_devices, dtype=jnp.int32) * TILE

    def one_block(block_start):
        out_cells = block_start + jnp.arange(y_block, dtype=jnp.int32)
        inner_cos, inner_sin = trig_table(out_cells, inner_cells, grid_columns)
        outer_cos, outer_sin = trig_table(out_cells, outer_cells, grid_columns)
        partial_sums = matmul(jnp.concatenate([inner_cos, inner_sin], 1), stacked_parts)
        partial_sums = partial_sums.reshape(y_block, 2, column_devices, items)
        real_sum = jnp.einsum(
            "ya,yan->yn", outer_cos, partial_sums[:, 0], precision=highest
        ) - jnp.einsum("ya,yan->yn", outer_sin, partial_sums[:, 1], precision=highest)
        imaginary_sum = jnp.einsum(
            "ya,yan->yn", outer_cos, partial_sums[:, 1], precision=highest
        ) + jnp.einsum("ya,yan->yn", outer_sin, partial_sums[:, 0], precision=highest)
        return jnp.stack([real_sum, imaginary_sum], 1)

    starts = jnp.arange(grid_columns // y_block, dtype=jnp.int32) * y_block
    moved = lax.map(one_block, starts).reshape(grid_columns, 2, 1, items)
    spectrum = lax.all_to_all(moved, "col", split_axis=0, concat_axis=2, tiled=True).reshape(
        TILE, 2, local_rows
    )
    real_rows = spectrum[:, 0, :].T
    imaginary_rows = spectrum[:, 1, :].T
    stacked_rows = jnp.concatenate(
        [
            jnp.concatenate([real_rows, -imaginary_rows], 0),
            jnp.concatenate([imaginary_rows, real_rows], 0),
        ],
        1,
    )
    row_cells = my_group * local_rows + jnp.arange(local_rows, dtype=jnp.int32)

    def sub_block(sub_start):
        out_cells = sub_start + jnp.arange(local_rows, dtype=jnp.int32)
        cosines, sines = trig_table(out_cells, row_cells, grid_rows)
        table = jnp.concatenate([cosines, sines], 1)
        return matmul(table, stacked_rows).reshape(local_rows, 2, TILE)

    starts = (
        jnp.arange(local_rows * lax.axis_size("tm") // local_rows, dtype=jnp.int32) * local_rows
    )
    image = lax.psum_scatter(
        lax.map(sub_block, starts).reshape(local_rows * lax.axis_size("tm"), 2, TILE),
        "tm",
        scatter_dimension=0,
        tiled=True,
    )
    x_cells = my_group * local_rows + jnp.arange(local_rows, dtype=jnp.int32)
    y_cells = my_column * TILE + jnp.arange(TILE, dtype=jnp.int32)
    real_out, imaginary_out = w_correct(
        image[:, 0, :], image[:, 1, :], x_cells, y_cells, w_plane[0], grid_rows, grid_columns
    )
    return (real_out, imaginary_out)


def solution(mesh):
    return jax.shard_map(
        shards,
        mesh=mesh,
        in_specs=(
            P("tm", "col", None, None),
            P("tm", "col", None, None),
            P("tm", "col"),
            P("tm", "col"),
            P(),
        ),
        out_specs=(P("tm", "col"), P("tm", "col")),
        check_vma=False,
    )
```

profile of v0, /device:TPU:1, one launch (start us, length us, event | category | flops | bytes accessed | tf_op | source)
XLA Modules:
  0.0 395.4 jit_solution(17200300209928324138)
XLA Ops:
  7.9 5.6 %copy.34 = f32[8,1,2,2048]{2,3,0,1:T(8,128)} copy(f32[8,1,2,2048]{3,2,1,0:T(2,128)} %param.11) | data formatting | bytes 262144 | tf_op args[0]
  13.6 2.4 broadcast_in_dim.52
  16.0 62.6 %while.40 = (s32[]{:T(128)}, f32[128,2,2048]{2,1,0:T(2,128)}, s32[]{:T(128)}, s32[8]{0:T(128)S(1)}, f32[8,2,2048]{2,0,1:T(8,128)S(1)}, /*index=5*/s32[]{:T(128)}...) while((s32[]{:T(128)}, f32[128,2,2048]{2,1,0:T(2,128)}, ...), condition=%wide.region_1.2_spmd.clone.clone, body=%wide.region_0.1_spmd.clone.clone.sunk | while | flops 278462592 | bytes 19072860 | solution.py:81
  17.4 1.7 fusion.81
  19.1 1.9 copy.89
  22.8 16.1 %broadcast_multiply_fusion.2 = bf16[2,2048,2,128]{3,2,1,0:T(2,128)(2,1)} fusion(f32[2,2048,128]{2,1,0:T(8,128)S(1)} %copy.89, f32[2,2048,2]{2,1,0:T(8,128)S(1)} %dynamic-slice_bitcast_fusion.6), kind=kLoop, calls=%fused_computation.25.clone.1 | loop fusion | flops 2097152 | bytes 4227072 | tf_op jit(solution)/shard_map/while/body/mul | solution.py:63
  38.8 3.2 mul.442
  50.5 1.9 copy.89
  54.1 16.1 %broadcast_multiply_fusion.2 = bf16[2,2048,2,128]{3,2,1,0:T(2,128)(2,1)} fusion(f32[2,2048,128]{2,1,0:T(8,128)S(1)} %copy.89, f32[2,2048,2]{2,1,0:T(8,128)S(1)} %dynamic-slice_bitcast_fusion.6), kind=kLoop, calls=%fused_computation.25.clone.1 | loop fusion | flops 2097152 | bytes 4227072 | tf_op jit(solution)/shard_map/while/body/mul | solution.py:63
  70.2 3.2 mul.442
  78.6 4.1 %copy.35 = f32[128,2,2048]{0,2,1:T(8,128)} copy(f32[128,2,2048]{2,1,0:T(2,128)} %get-tuple-element.192) | data formatting | bytes 4194304 | tf_op jit(solution)/shard_map/while | solution.py:81
  82.7 113.0 %reduce-scatter.3.cloned.1.call-done = f32[128,2,256]{0,2,1:T(8,128)} async-done(((f32[128,2,2048]{0,2,1:T(8,128)}), f32[128,2,256]{0,2,1:T(8,128)}) %reduce-scatter.3.cloned.1.call-update) | async-done | bytes 262160 | tf_op jit(solution)/shard_map/reduce_scatter | solution.py:93
  197.4 9.5 %all-to-all-start = ((f32[128,2,32,8]{0,3,1,2:T(8,128)}), f32[128,2,32,8]{0,3,1,2:T(8,128)S(1)}, u32[]{:S(2)}, u32[]{:S(2)}) async-start(f32[128,2,32,8]{0,3,1,2:T(8,128)} %copy.36), calls=%async_computation.1 | async-start | bytes 524288 | tf_op jit(solution)/shard_map/all_to_all | solution.py:102
  206.9 13.0 %all-to-all-done = f32[128,2,32,8]{0,3,1,2:T(8,128)S(1)} async-done(((f32[128,2,32,8]{0,3,1,2:T(8,128)}), f32[128,2,32,8]{0,3,1,2:T(8,128)S(1)}, u32[]{:S(2)}, u32[]{:S(2)}) %all-to-all-start) | async-done | bytes 262176 | tf_op jit(solution)/shard_map/all_to_all | solution.py:102
  220.6 38.9 %while.38 = (s32[]{:T(128)}, f32[8,512,2,8]{1,3,2,0:T(8,128)S(1)}, s32[8]{0:T(128)S(1)}, f32[256,512]{1,0:T(8,128)S(1)}, s32[]{:T(128)}) while((s32[]{:T(128)}, f32[8,512,2,8]{1,3,2,0:T(8,128)S(1)}, s32[8]{0:T(128)S(1)}, f32[256,512]{1,0:T(8,128)S(1)}, s32[]{:T(128)}) %tuple.116), condition=%wide.region_4.5_spmd.clone, body=%wide.region_3.4_spmd.clone.sunk | while | flops 807633408 | bytes 4430161 | solution.py:141
  259.5 4.3 %copy.66 = f32[8,512,2,8]{3,2,1,0:T(2,128)} copy(f32[8,512,2,8]{1,3,2,0:T(8,128)S(1)} %get-tuple-element.193) | data formatting | bytes 524288 | tf_op jit(solution)/shard_map/reshape | solution.py:141
  263.8 7.8 %reshape.125 = f32[32,1,2048]{2,1,0:T(1,128)} reshape(f32[4096,1,2,8]{3,2,1,0:T(2,128)} %bitcast.123) | data formatting | bytes 524288
  271.6 4.5 %all-to-all-start.1 = ((f32[32,1,2048]{2,1,0:T(1,128)}), f32[32,1,2048]{2,1,0:T(1,128)S(1)}, u32[]{:S(2)}, u32[]{:S(2)}) async-start(f32[32,1,2048]{2,1,0:T(1,128)} %reshape.125), calls=%async_computation.2 | async-start | bytes 524288 | tf_op jit(solution)/shard_map/all_to_all | solution.py:142
  276.4 12.6 %all-to-all-done.1 = f32[32,1,2048]{2,1,0:T(1,128)S(1)} async-done(((f32[32,1,2048]{2,1,0:T(1,128)}), f32[32,1,2048]{2,1,0:T(1,128)S(1)}, u32[]{:S(2)}, u32[]{:S(2)}) %all-to-all-start.1) | async-done | bytes 262176 | tf_op jit(solution)/shard_map/all_to_all | solution.py:142
  290.7 7.7 %reshape.126 = f32[4096,1,2,8]{3,2,1,0:T(2,128)} reshape(f32[32,2048]{1,0:T(8,128)S(1)} %reduce.8) | data formatting | bytes 524288
  298.4 5.1 %copy.43 = f32[4096,2,1,8]{0,2,3,1:T(1,128)S(1)} copy(f32[4096,2,1,8]{3,1,2,0:T(2,128)} %bitcast.124) | data formatting | bytes 524288 | tf_op jit(solution)/shard_map/all_to_all | solution.py:142
  303.8 33.7 %while.39 = (s32[]{:T(128)}, f32[8,256,2,128]{3,1,0,2:T(8,128)}, s32[8]{0:T(128)S(1)}, f32[512,256]{1,0:T(8,128)S(1)}, s32[]{:T(128)}, /*index=5*/s32[]{:T(128)}) while((s32[]{:T(128)}, f32[8,256,2,128]{3,1,0,2:T(8,128)}, s32[8]{0:T(128)S(1)}, f32[512,256]{1,0:T(8,128)S(1)}, s32[]{:T(128)}, /*index=5*/s32[]{:T(128)}) %tuple.119), condition=%wide.region_6.7_spmd.clone, body=%wide.region_5.6_spmd.clone.sunk | while | flops 403702272 | bytes 2888281 | solution.py:166
  338.2 48.1 %reduce-scatter.5.cloned.1.call-done = f32[256,2,128]{2,0,1:T(8,128)} async-done(((f32[2048,2,128]{2,0,1:T(8,128)}), f32[256,2,128]{2,0,1:T(8,128)}) %reduce-scatter.5.cloned.1.call-update) | async-done | bytes 262160 | tf_op jit(solution)/shard_map/reduce_scatter | solution.py:165
  386.3 2.3 add_multiply_fusion
  (189 shorter events, 92.5 us)
Async XLA Ops:
  7.2 188.5 %reduce-scatter.3.cloned.1.call-start = ((), (), s32[]{:S(2)}) async-start(), calls=%async_computation.4 | async-start | bytes 2359296 | tf_op jit(solution)/shard_map/reduce_scatter | solution.py:93
  7.9 5.6 %copy-start = (f32[8,1,2,2048]{3,2,1,0:T(2,128)S(1)}, f32[8,1,2,2048]{3,2,1,0:T(2,128)}, u32[]{:S(2)}) copy-start(f32[8,1,2,2048]{3,2,1,0:T(2,128)} %param.12) | copy-start | bytes 393220
  13.5 2.5 copy-start.1
  197.4 22.6 %all-to-all-start = ((f32[128,2,32,8]{0,3,1,2:T(8,128)}), f32[128,2,32,8]{0,3,1,2:T(8,128)S(1)}, u32[]{:S(2)}, u32[]{:S(2)}) async-start(f32[128,2,32,8]{0,3,1,2:T(8,128)} %copy.36), calls=%async_computation.1 | async-start | bytes 524288 | tf_op jit(solution)/shard_map/all_to_all | solution.py:102
  271.6 17.3 %all-to-all-start.1 = ((f32[32,1,2048]{2,1,0:T(1,128)}), f32[32,1,2048]{2,1,0:T(1,128)S(1)}, u32[]{:S(2)}, u32[]{:S(2)}) async-start(f32[32,1,2048]{2,1,0:T(1,128)} %reshape.125), calls=%async_computation.2 | async-start | bytes 524288 | tf_op jit(solution)/shard_map/all_to_all | solution.py:142
  276.1 110.2 %reduce-scatter.5.cloned.1.call-start = ((), (), s32[]{:S(2)}) async-start(), calls=%async_computation.5 | async-start | bytes 2359296 | tf_op jit(solution)/shard_map/reduce_scatter | solution.py:165
Sparse Core Ops, SparseCore 0:
  82.8 112.8 reduce-scatter.2
  337.6 48.6 reduce-scatter.4
where the time goes:
time: 401 us; the launch traced here: 395 us
  waiting for transfers between devices  187 us (47%)
  other arithmetic  84.8 us (21%)
  local copies, waits for them, and re-layouts  72.9 us (18%)
  matrix products  17.7 us (4%)
  between operations  15.5 us (4%)
  starting transfers between devices  14.3 us (4%)
    reduce_scatter x1, waiting for transfers between devices, shards(): local_grid = lax.psum_scatter(grid, 'tm', scatter_dimension=2, tiled=True)  113 us
    reduce_scatter x1, waiting for transfers between devices, shards(): lax.psum_scatter(lax.map(sub_block, starts).reshape(local_rows * lax.axis...  48.1 us
    mul x2, other arithmetic, one_turn(): jnp.swapaxes(value_pair, 1, 2)[:, :, :, None]  32.1 us
    cos x24, other arithmetic, trig_table(): return (jnp.cos(angle), jnp.sin(angle))  26.3 us
    unnamed x9, local copies, waits for them, and re-layouts  21.4 us
    dot_general x16, matrix products, matmul(): jnp.dot(left, right, precision=highest, preferred_element_type=jnp.float32)  16.5 us
    all_to_all x1, waiting for transfers between devices, shards(): lax.all_to_all(split_grid, 'col', split_axis=2, concat_axis=0, tiled=True)  13 us
    all_to_all x1, waiting for transfers between devices, shards(): lax.all_to_all(moved, 'col', split_axis=0, concat_axis=2, tiled=True)  12.6 us
  transfers between devices with their start and end apart: 4, of which 4 were waited for; matrix products, arithmetic and copies ran while one was open for 0% of the time, Pallas kernels for 0%

commit v1 on v0

v1 whole, which is shorter than its diff:
```python
import math

import jax
import jax.numpy as jnp
import numpy as np
from jax import lax
from jax.experimental import pallas as pl
from jax.experimental.pallas import tpu as pltpu
from jax.sharding import PartitionSpec as P

TILE = 128
TROWS = 16
NU = 2048
NV = 4096
GROUPS = 8
COLUMNS = 32
SLOTS = 8
BLOCK = 2048
PART = TILE // GROUPS
CHUNK = 512

f32 = jnp.float32
bf16 = jnp.bfloat16
NT = (((1,), (1,)), ((), ()))
NN = (((1,), (0,)), ((), ()))


def unit(product, length):
    angle = np.mod(product, length) * (2.0 * math.pi / length)
    return np.cos(angle), np.sin(angle)


def split(table):
    table = np.asarray(table, np.float32)
    high = table.astype(jnp.bfloat16)
    low = (table - high.astype(np.float32)).astype(jnp.bfloat16)
    return np.stack([high, low])


def inner_u_table():
    x2 = np.arange(TILE)[:, None]
    i = np.arange(TILE)[None, :]
    c, s = unit(x2 * i, TILE)
    return split(np.block([[c, -s], [s, c]]))


def twiddle_u_table():
    x1 = np.arange(TROWS)[:, None]
    i = np.arange(TILE)[None, :]
    c, s = unit(x1 * i, NU)
    return np.stack([c, s], 1).astype(np.float32)


def column_table():
    y1 = np.arange(COLUMNS)[:, None]
    c = np.arange(COLUMNS)[None, :]
    tables = []
    for g in range(GROUPS):
        co, si = unit(TILE * c * y1 + PART * g * y1, NV)
        t = np.zeros((2, COLUMNS, COLUMNS, 2))
        t[0, :, :, 0], t[0, :, :, 1] = co, -si
        t[1, :, :, 0], t[1, :, :, 1] = si, co
        tables.append(t.reshape(2 * COLUMNS, 2 * COLUMNS))
    return split(np.stack(tables))


def twiddle_v_table():
    ya = np.arange(GROUPS)[:, None, None]
    y1 = np.arange(COLUMNS)[None, :, None]
    j = (np.arange(TILE) % PART)[None, None, :]
    c, s = unit(j * (y1 + COLUMNS * ya), NV)
    return np.stack([c, s], 1).astype(np.float32)


def inner_v_table():
    yb = np.arange(PART)[:, None]
    j = np.arange(PART)[None, :]
    c, s = unit(yb * j, PART)
    t = np.zeros((PART, 2, 8, 2, 8, PART))
    for xx in range(8):
        t[:, 0, xx, 0, xx, :] = c
        t[:, 0, xx, 1, xx, :] = -s
        t[:, 1, xx, 0, xx, :] = s
        t[:, 1, xx, 1, xx, :] = c
    return split(t.reshape(256, 256))


def dot3(a_high, a_low, b, dims):
    b_high = b.astype(bf16)
    b_low = (b - b_high.astype(f32)).astype(bf16)
    def dot(x, y):
        return lax.dot_general(x, y, dims, preferred_element_type=f32)
    return dot(a_high, b_high) + (dot(a_low, b_high) + dot(a_high, b_low))


def fft(items):
    n = len(items)
    if n == 1:
        return items
    even = fft(items[0::2])
    odd = fft(items[1::2])
    out = [None] * n
    for k in range(n // 2):
        er, ei = even[k]
        a, b = odd[k]
        if k == 0:
            tr, ti = a, b
        elif 4 * k == n:
            tr, ti = -b, a
        elif 8 * k == n:
            h = math.sqrt(0.5)
            tr, ti = (a - b) * h, (a + b) * h
        elif 8 * k == 3 * n:
            h = math.sqrt(0.5)
            tr, ti = (a + b) * -h, (a - b) * h
        else:
            c, s = math.cos(2 * math.pi * k / n), math.sin(2 * math.pi * k / n)
            tr, ti = a * c - b * s, a * s + b * c
        out[k] = (er + tr, ei + ti)
        out[k + n // 2] = (er - tr, ei - ti)
    return out


def grid_kernel(count_ref, row_ref, vis_ref, place_ref, out_ref):
    count = count_ref[0, 0]
    cells = lax.broadcasted_iota(jnp.int32, (TILE, CHUNK), 0).astype(f32)

    def taper(position):
        offset = cells - position
        inside = jnp.maximum(1.0 - offset * offset, 0.0)
        return (inside * inside).astype(bf16)

    def one_slot(slot, carry):
        total = jnp.zeros((TILE, 2 * TILE), f32)
        for start in range(0, BLOCK, CHUNK):
            at = pl.ds(start, CHUNK)
            weight_u = taper(place_ref[slot, 0, 0:1, at]).astype(f32)
            weight_v = taper(place_ref[slot, 0, 1:2, at])
            real = (weight_u * vis_ref[slot, 0, 0:1, at]).astype(bf16)
            imaginary = (weight_u * vis_ref[slot, 0, 1:2, at]).astype(bf16)
            weighted = jnp.concatenate([real, imaginary], 0)
            total += lax.dot_general(weight_v, weighted, NT, preferred_element_type=f32)
        for part in range(2):
            piece = total[:, part * TILE : (part + 1) * TILE].reshape(GROUPS, PART, TILE)
            first = pl.multiple_of(slot * (2 * PART) + part * PART, PART)
            out_ref[:, pl.ds(first, PART), :] = piece
        return carry

    lax.fori_loop(0, count, one_slot, 0)
    slot_of = lax.broadcasted_iota(jnp.int32, (SLOTS, TILE), 0)
    label = jnp.full((SLOTS, TILE), TROWS, jnp.int32)
    for slot in range(SLOTS):
        here = jnp.where(slot < count, row_ref[slot, 0], TROWS)
        label = jnp.where(slot_of == slot, here, label)
    label = label.astype(f32)
    for g in range(GROUPS):
        out_ref[g, 2 * PART * SLOTS :, :] = label


def transform_u_kernel(label_ref, piece_ref, table_ref, twiddle_ref, out_ref, grid_ref, rows_ref):
    grid_ref[...] = jnp.zeros_like(grid_ref)
    for t in range(GROUPS):
        for slot in range(SLOTS):
            row = label_ref[t, slot, 0].astype(jnp.int32)
            grid_ref[row] += piece_ref[t, 2 * PART * slot : 2 * PART * (slot + 1), :]
    items = [(grid_ref[r, :PART, :], grid_ref[r, PART:, :]) for r in range(TROWS)]
    for x1, (a, b) in enumerate(fft(items)):
        c = twiddle_ref[x1, 0:1, :]
        s = twiddle_ref[x1, 1:2, :]
        rows_ref[x1 * PART : (x1 + 1) * PART, :TILE] = a * c - b * s
        rows_ref[x1 * PART : (x1 + 1) * PART, TILE:] = a * s + b * c
    out = dot3(table_ref[0], table_ref[1], rows_ref[...], NT)
    for half in range(2):
        for part in range(2):
            out_ref[pl.ds(2 * half + part, TILE, stride=4), :] = out[
                part * TILE : (part + 1) * TILE, half * TILE : (half + 1) * TILE
            ]


def transform_v_kernel(data_ref, column_ref, twiddle_ref, table_ref, out_ref, rows_ref):
    items = []
    for g in range(GROUPS):
        u = dot3(column_ref[0, g], column_ref[1, g], data_ref[64 * g : 64 * (g + 1), :], NN)
        items.append((u[:COLUMNS], u[COLUMNS:]))
    for ya, (a, b) in enumerate(fft(items)):
        c = twiddle_ref[ya, 0]
        s = twiddle_ref[ya, 1]
        rows_ref[ya * COLUMNS : (ya + 1) * COLUMNS, :TILE] = a * c - b * s
        rows_ref[ya * COLUMNS : (ya + 1) * COLUMNS, TILE:] = a * s + b * c
    out = dot3(table_ref[0], table_ref[1], rows_ref[...], NT)
    for yb in range(PART):
        for half in range(2):
            out_ref[2 * yb + half] = out[
                yb * 16 : (yb + 1) * 16, half * TILE : (half + 1) * TILE
            ]


def correct_kernel(index_ref, plane_ref, data_ref, real_ref, imaginary_ref):
    rows = real_ref.shape[0]
    x = lax.broadcasted_iota(jnp.int32, (rows, TILE), 0) + index_ref[0] * rows
    y = lax.broadcasted_iota(jnp.int32, (rows, TILE), 1) + index_ref[1] * TILE
    along_l = (x - NU // 2).astype(f32) * (1.0 / NU)
    along_m = (y - NV // 2).astype(f32) * (1.0 / NV)
    height = jnp.sqrt(1.0 - along_l * along_l - along_m * along_m)
    phase = 2.0 * math.pi * plane_ref[0] * (height - 1.0)
    scale = 1.0 / math.sqrt(NU * NV)
    cosine = jnp.cos(phase) * scale
    sine = jnp.sin(phase) * scale
    a = data_ref[:, :8, :].reshape(rows, TILE)
    b = data_ref[:, 8:, :].reshape(rows, TILE)
    real_ref[...] = a * cosine - b * sine
    imaginary_ref[...] = a * sine + b * cosine


VMEM = pl.BlockSpec(memory_space=pltpu.VMEM)
SMEM = pl.BlockSpec(memory_space=pltpu.SMEM)


def call(kernel, outs, in_specs, scratch=(), grid=()):
    single = not isinstance(outs, list)
    return pl.pallas_call(
        kernel,
        out_shape=outs,
        grid=grid,
        in_specs=in_specs,
        out_specs=VMEM if single else [VMEM] * len(outs),
        scratch_shapes=list(scratch),
        compiler_params=pltpu.CompilerParams(vmem_limit_bytes=32 * 1024 * 1024),
    )


def shards(visibilities, coords, tile_row, counts, w_plane):
    def shape(*dims):
        return jax.ShapeDtypeStruct(dims, f32)

    length = 2 * PART * SLOTS + SLOTS
    pieces = call(grid_kernel, shape(GROUPS, length, TILE), [SMEM, SMEM, VMEM, VMEM])(
        counts, tile_row, visibilities, coords
    )
    pieces = lax.all_to_all(pieces, "tm", 0, 0, tiled=True)
    label_spec = pl.BlockSpec(
        (GROUPS, SLOTS, TILE), lambda step: (0, 2 * PART, 0), memory_space=pltpu.SMEM
    )
    spectrum = call(
        transform_u_kernel,
        shape(512, TILE),
        [label_spec, VMEM, VMEM, VMEM],
        [pltpu.VMEM((TROWS + 1, 2 * PART, TILE), f32), pltpu.VMEM((256, 256), f32)],
        (1,),
    )(pieces, pieces, jnp.asarray(inner_u_table()), jnp.asarray(twiddle_u_table()))
    spectrum = lax.all_to_all(
        spectrum.reshape(256, 2, TILE), ("tm", "col"), 0, 0, tiled=True
    ).reshape(512, TILE)
    image = call(
        transform_v_kernel,
        shape(COLUMNS, 16, TILE),
        [VMEM, VMEM, VMEM, VMEM],
        [pltpu.VMEM((256, 256), f32)],
    )(
        spectrum,
        jnp.asarray(column_table()),
        jnp.asarray(twiddle_v_table()),
        jnp.asarray(inner_v_table()),
    )
    image = lax.all_to_all(image, "col", 0, 0, tiled=True)
    index = jnp.stack([lax.axis_index("tm"), lax.axis_index("col")]).astype(jnp.int32)
    rows = NU // GROUPS
    return tuple(
        call(correct_kernel, [shape(rows, TILE)] * 2, [SMEM, SMEM, VMEM])(index, w_plane, image)
    )


def solution(mesh):
    return jax.shard_map(
        shards,
        mesh=mesh,
        in_specs=(
            P("tm", "col", None, None),
            P("tm", "col", None, None),
            P("tm", "col"),
            P("tm", "col"),
            P(),
        ),
        out_specs=(P("tm", "col"), P("tm", "col")),
        check_vma=False,
    )
```

time: 401 us -> 79.6 us (0.20); the launches traced: 395 us -> 79.6 us
  waiting for transfers between devices: 187 us -> 12.8 us
  other arithmetic: 84.8 us -> 0.08 us
  local copies, waits for them, and re-layouts: 72.9 us -> 2.56 us
  blocking collectives: 0 us -> 51.2 us
  matrix products: 17.7 us -> 0 us
  between operations: 15.5 us -> 2 us
  starting transfers between devices: 14.3 us -> 3.99 us
  Pallas kernels: 0 us -> 6.94 us
    reduce_scatter x2 -> x0, waiting for transfers between devices: 161 us -> none  [the longest x1 113 us: shards(): local_grid = lax.psum_scatter(grid, 'tm', scatter_dimension=2, tiled=True)]
    all_to_all x0 -> x2, blocking collectives: none -> 51.2 us  [the longest x1 31.3 us: shards(): lax.all_to_all(spectrum.reshape(256, 2, TILE), ('tm', 'col'), 0, 0, tiled...]
    mul x14 -> x0, other arithmetic: 34.4 us -> none  [the longest x2 32.1 us: one_turn(): jnp.swapaxes(value_pair, 1, 2)[:, :, :, None]]
    cos x24 -> x0, other arithmetic: 26.3 us -> none  [trig_table(): return (jnp.cos(angle), jnp.sin(angle))]
    unnamed x9 -> x15, local copies, waits for them, and re-layouts: 21.4 us -> 2.56 us
    dot_general x18 -> x0, matrix products: 17.7 us -> none  [the longest x16 16.5 us: matmul(): jnp.dot(left, right, precision=highest, preferred_element_type=jnp.float32)]
    all_to_all x2 -> x1, waiting for transfers between devices: 25.6 us -> 12.8 us  [shards(): image = lax.all_to_all(image, 'col', 0, 0, tiled=True)]
    all_to_all x2 -> x1, starting transfers between devices: 14 us -> 3.99 us  [shards(): image = lax.all_to_all(image, 'col', 0, 0, tiled=True)]
  transfers between devices with their start and end apart: 4 -> 1, of which waited for: 4 -> 1; matrix products, arithmetic and copies ran while one was open for 0% -> 0% of each run, Pallas kernels for 0% -> 0%
where the time goes in v1:
time: 79.6 us
  blocking collectives  51.2 us (64%)
  waiting for transfers between devices  12.8 us (16%)
  Pallas kernels  6.94 us (9%)
  starting transfers between devices  3.99 us (5%)
  local copies, waits for them, and re-layouts  2.56 us (3%)
  between operations  2 us (3%)
    all_to_all x1, blocking collectives, shards(): lax.all_to_all(spectrum.reshape(256, 2, TILE), ('tm', 'col'), 0, 0, tiled...  31.3 us
    all_to_all x1, blocking collectives, shards(): pieces = lax.all_to_all(pieces, 'tm', 0, 0, tiled=True)  19.9 us
    all_to_all x1, waiting for transfers between devices, shards(): image = lax.all_to_all(image, 'col', 0, 0, tiled=True)  12.8 us
    all_to_all x1, starting transfers between devices, shards(): image = lax.all_to_all(image, 'col', 0, 0, tiled=True)  3.99 us
    unnamed x15, local copies, waits for them, and re-layouts  2.56 us
    pallas_call x1, Pallas kernels, shards(): call(grid_kernel, shape(GROUPS, length, TILE), [SMEM, SMEM, VMEM, VMEM])  1.98 us
    pallas_call x1, Pallas kernels, shards(): call(correct_kernel, [shape(rows, TILE)] * 2, [SMEM, SMEM, VMEM])  1.83 us
    pallas_call x1, Pallas kernels, shards(): call(transform_u_kernel, shape(512, TILE), [label_spec, VMEM, VMEM, VMEM]...  1.82 us
  transfers between devices with their start and end apart: 1, of which 1 were waited for; matrix products, arithmetic and copies ran while one was open for 0% of the time, Pallas kernels for 0%

profile of v1, /device:TPU:1, one launch (start us, length us, event | category | flops | bytes accessed | tf_op | source)
XLA Modules:
  0.0 79.6 jit_solution(14486612157589846935)
XLA Ops:
  0.6 0.7 copy.12.row_ref
  2.0 0.0 copy-start.4
  2.0 0.9 %copy-done.4 = f32[8,1,2,2048]{3,2,1,0:T(2,128)S(1)} copy-done((f32[8,1,2,2048]{3,2,1,0:T(2,128)S(1)}, f32[8,1,2,2048]{3,2,1,0:T(2,128)}, u32[]{:S(2)}) %copy-start.4) | copy-done | bytes 131096
  2.9 0.0 copy-start.5
  2.9 0.9 %copy-done.5 = f32[8,1,2,2048]{3,2,1,0:T(2,128)S(1)} copy-done((f32[8,1,2,2048]{3,2,1,0:T(2,128)S(1)}, f32[8,1,2,2048]{3,2,1,0:T(2,128)}, u32[]{:S(2)}) %copy-start.5) | copy-done | bytes 131096
  3.8 2.0 %shard_map.113 = f32[8,264,128]{2,1,0:T(8,128)S(1)} custom-call(s32[1,1]{1,0:T(1,128)S(6)} %copy.13.count_ref, s32[8,1]{1,0:T(8,128)S(1)} %copy.12.row_ref, f32[8,1,2,2048]{3,2,1,0:T(2,128)S(1)} %copy-done.4, f32[8,1,2,2048]{3,2,1,0:T(2,128)S(1)} %copy-done.5), custom_call_target="tpu_custom_call" | custom-call | tf_op jit(solution)/shard_map/pallas_call | solution.py:237
  5.8 0.0 copy-start.3
  5.8 0.0 copy-start.6
  5.8 19.9 %all_to_all.15.label_ref.piece_ref = f32[8,264,128]{2,1,0:T(8,128)S(1)} all-to-all(f32[8,264,128]{2,1,0:T(8,128)S(1)} %shard_map.113), channel_id=1, replica_groups=mesh['tm'=8,'col'=32] {'tm'}, dimensions={0} | all-to-all | bytes 2162688 | tf_op jit(solution)/shard_map/all_to_all | solution.py:240
  25.8 0.0 copy-done.3
  25.8 0.0 copy-done.6
  25.8 0.0 copy-start
  25.8 0.0 copy-start.1
  25.8 0.0 copy-start.2
  25.8 1.8 %shard_map.114 = f32[512,128]{1,0:T(8,128)S(1)} custom-call(f32[8,264,128]{2,1,0:T(8,128)S(1)} %all_to_all.15.label_ref.piece_ref, f32[8,264,128]{2,1,0:T(8,128)S(1)} %all_to_all.15.label_ref.piece_ref, bf16[2,256,256]{2,1,0:T(8,128)(2,1)S(1)} %copy-done.3, f32[16,2,128]{2,1,0:T(2,128)S(1)} %copy-done.6), custom_call_target="tpu_custom_call" | custom-call | tf_op jit(solution)/shard_map/pallas_call | solution.py:244
  27.6 31.3 %all_to_all.16 = f32[256,2,128]{2,1,0:T(2,128)S(1)} all-to-all(f32[256,2,128]{2,1,0:T(2,128)S(1)} %bitcast.5), channel_id=1, replica_groups=mesh['tm'=8,'col'=32] {'tm','col'}, dimensions={0} | all-to-all | bytes 524288 | tf_op jit(solution)/shard_map/all_to_all | solution.py:251
  58.9 0.0 copy-done
  58.9 0.0 copy-done.1
  58.9 0.0 copy-done.2
  58.9 1.3 %shard_map.115 = f32[32,16,128]{2,1,0:T(8,128)} custom-call(f32[512,128]{1,0:T(8,128)S(1)} %bitcast.4, bf16[2,8,64,64]{3,2,1,0:T(8,128)(2,1)S(1)} %copy-done, f32[8,2,32,128]{3,2,1,0:T(8,128)S(1)} %copy-done.1, bf16[2,256,256]{2,1,0:T(8,128)(2,1)S(1)} %copy-done.2), custom_call_target="tpu_custom_call" | custom-call | tf_op jit(solution)/shard_map/pallas_call | solution.py:254
  60.2 4.0 %all-to-all-start.2 = ((f32[32,16,128]{2,1,0:T(8,128)}), f32[32,16,128]{2,1,0:T(8,128)S(1)}, u32[]{:S(2)}, u32[]{:S(2)}) async-start(f32[32,16,128]{2,1,0:T(8,128)} %shard_map.115), calls=%async_computation.2 | async-start | bytes 524288 | tf_op jit(solution)/shard_map/all_to_all | solution.py:265
  64.9 0.1 pad_add_fusion.index_ref
  65.0 12.8 %all-to-all-done.2.data_ref = f32[32,16,128]{2,1,0:T(8,128)S(1)} async-done(((f32[32,16,128]{2,1,0:T(8,128)}), f32[32,16,128]{2,1,0:T(8,128)S(1)}, u32[]{:S(2)}, u32[]{:S(2)}) %all-to-all-start.2) | async-done | bytes 262176 | tf_op jit(solution)/shard_map/all_to_all | solution.py:265
  77.8 1.8 %shard_map.116 = (f32[256,128]{1,0:T(8,128)}, f32[256,128]{1,0:T(8,128)}) custom-call(s32[2]{0:T(128)S(1)} %pad_add_fusion.index_ref, f32[1]{0:T(128)S(6)} %copy.14.plane_ref, f32[32,16,128]{2,1,0:T(8,128)S(1)} %all-to-all-done.2.data_ref), custom_call_target="tpu_custom_call" | custom-call | tf_op jit(solution)/shard_map/pallas_call | solution.py:269
Async XLA Ops:
  2.0 0.9 %copy-start.4 = (f32[8,1,2,2048]{3,2,1,0:T(2,128)S(1)}, f32[8,1,2,2048]{3,2,1,0:T(2,128)}, u32[]{:S(2)}) copy-start(f32[8,1,2,2048]{3,2,1,0:T(2,128)} %vis_ref.1) | copy-start | bytes 393220
  2.9 0.9 %copy-start.5 = (f32[8,1,2,2048]{3,2,1,0:T(2,128)S(1)}, f32[8,1,2,2048]{3,2,1,0:T(2,128)}, u32[]{:S(2)}) copy-start(f32[8,1,2,2048]{3,2,1,0:T(2,128)} %place_ref.1) | copy-start | bytes 393220
  5.8 19.9 %copy-start.3 = (bf16[2,256,256]{2,1,0:T(8,128)(2,1)S(1)}, bf16[2,256,256]{2,1,0:T(8,128)(2,1)}, u32[]{:S(2)}) copy-start(bf16[2,256,256]{2,1,0:T(8,128)(2,1)} %constant.19.clone.table_ref) | copy-start | bytes 786436
  5.8 19.9 %copy-start.6 = (f32[16,2,128]{2,1,0:T(2,128)S(1)}, f32[16,2,128]{2,1,0:T(2,128)}, u32[]{:S(2)}) copy-start(f32[16,2,128]{2,1,0:T(2,128)} %constant.20.clone.twiddle_ref) | copy-start | bytes 49156
  25.8 33.2 %copy-start = (bf16[2,8,64,64]{3,2,1,0:T(8,128)(2,1)S(1)}, bf16[2,8,64,64]{3,2,1,0:T(8,128)(2,1)}, u32[]{:S(2)}) copy-start(bf16[2,8,64,64]{3,2,1,0:T(8,128)(2,1)} %constant.21.clone.column_ref) | copy-start | bytes 393220
  25.8 33.2 %copy-start.1 = (f32[8,2,32,128]{3,2,1,0:T(8,128)S(1)}, f32[8,2,32,128]{3,2,1,0:T(8,128)}, u32[]{:S(2)}) copy-start(f32[8,2,32,128]{3,2,1,0:T(8,128)} %constant.22.clone.twiddle_ref) | copy-start | bytes 786436
  25.8 33.2 %copy-start.2 = (bf16[2,256,256]{2,1,0:T(8,128)(2,1)S(1)}, bf16[2,256,256]{2,1,0:T(8,128)(2,1)}, u32[]{:S(2)}) copy-start(bf16[2,256,256]{2,1,0:T(8,128)(2,1)} %constant.23.clone.table_ref) | copy-start | bytes 786436
  60.2 17.6 %all-to-all-start.2 = ((f32[32,16,128]{2,1,0:T(8,128)}), f32[32,16,128]{2,1,0:T(8,128)S(1)}, u32[]{:S(2)}, u32[]{:S(2)}) async-start(f32[32,16,128]{2,1,0:T(8,128)} %shard_map.115), calls=%async_computation.2 | async-start | bytes 524288 | tf_op jit(solution)/shard_map/all_to_all | solution.py:265

commit v2 on v1

--- a/solution.py
+++ b/solution.py
@@ -121,8 +121,38 @@
     return out
 
 
-def grid_kernel(count_ref, row_ref, vis_ref, place_ref, out_ref):
+def grid_kernel(
+    count_ref, row_hbm, vis_hbm, place_hbm, out_ref, row_ref, vis_ref, place_ref, known, arrived
+):
+    rows = pltpu.make_async_copy(row_hbm, row_ref, known)
+    rows.start()
+
+    def fetch(slot):
+        return (
+            pltpu.make_async_copy(vis_hbm.at[slot, 0], vis_ref.at[slot], arrived.at[0, slot]),
+            pltpu.make_async_copy(place_hbm.at[slot, 0], place_ref.at[slot], arrived.at[1, slot]),
+        )
+
+    for slot in range(SLOTS):
+        for copy in fetch(slot):
+            copy.start()
+
+    def wait(slot, carry):
+        for copy in fetch(slot):
+            copy.wait()
+        return carry
+
+    rows.wait()
     count = count_ref[0, 0]
+    slot_of = lax.broadcasted_iota(jnp.int32, (SLOTS, TILE), 0)
+    label = jnp.full((SLOTS, TILE), TROWS, jnp.int32)
+    for slot in range(SLOTS):
+        here = jnp.where(slot < count, row_ref[0, slot], TROWS)
+        label = jnp.where(slot_of == slot, here, label)
+    label = label.astype(f32)
+    for g in range(GROUPS):
+        out_ref[g, 2 * PART * SLOTS :, :] = label
+
     cells = lax.broadcasted_iota(jnp.int32, (TILE, CHUNK), 0).astype(f32)
 
     def taper(position):
@@ -131,13 +161,14 @@
         return (inside * inside).astype(bf16)
 
     def one_slot(slot, carry):
+        wait(slot, 0)
         total = jnp.zeros((TILE, 2 * TILE), f32)
         for start in range(0, BLOCK, CHUNK):
             at = pl.ds(start, CHUNK)
-            weight_u = taper(place_ref[slot, 0, 0:1, at]).astype(f32)
-            weight_v = taper(place_ref[slot, 0, 1:2, at])
-            real = (weight_u * vis_ref[slot, 0, 0:1, at]).astype(bf16)
-            imaginary = (weight_u * vis_ref[slot, 0, 1:2, at]).astype(bf16)
+            weight_u = taper(place_ref[slot, 0:1, at])
+            weight_v = taper(place_ref[slot, 1:2, at])
+            real = weight_u * vis_ref[slot, 0:1, at].astype(bf16)
+            imaginary = weight_u * vis_ref[slot, 1:2, at].astype(bf16)
             weighted = jnp.concatenate([real, imaginary], 0)
             total += lax.dot_general(weight_v, weighted, NT, preferred_element_type=f32)
         for part in range(2):
@@ -147,23 +178,18 @@
         return carry
 
     lax.fori_loop(0, count, one_slot, 0)
-    slot_of = lax.broadcasted_iota(jnp.int32, (SLOTS, TILE), 0)
-    label = jnp.full((SLOTS, TILE), TROWS, jnp.int32)
-    for slot in range(SLOTS):
-        here = jnp.where(slot < count, row_ref[slot, 0], TROWS)
-        label = jnp.where(slot_of == slot, here, label)
-    label = label.astype(f32)
-    for g in range(GROUPS):
-        out_ref[g, 2 * PART * SLOTS :, :] = label
-
-
-def transform_u_kernel(label_ref, piece_ref, table_ref, twiddle_ref, out_ref, grid_ref, rows_ref):
+    lax.fori_loop(count, SLOTS, wait, 0)
+
+
+def transform_u_kernel(piece_ref, table_ref, twiddle_ref, out_ref, grid_ref, rows_ref):
     grid_ref[...] = jnp.zeros_like(grid_ref)
     for t in range(GROUPS):
+        label = piece_ref[t, 2 * PART * SLOTS :, :].astype(jnp.int32)
         for slot in range(SLOTS):
-            row = label_ref[t, slot, 0].astype(jnp.int32)
-            grid_ref[row] += piece_ref[t, 2 * PART * slot : 2 * PART * (slot + 1), :]
-    items = [(grid_ref[r, :PART, :], grid_ref[r, PART:, :]) for r in range(TROWS)]
+            row = label[slot, 0]
+            grid_ref[slot % 2, row] += piece_ref[t, 2 * PART * slot : 2 * PART * (slot + 1), :]
+    cells = [grid_ref[0, r] + grid_ref[1, r] for r in range(TROWS)]
+    items = [(cell[:PART], cell[PART:]) for cell in cells]
     for x1, (a, b) in enumerate(fft(items)):
         c = twiddle_ref[x1, 0:1, :]
         s = twiddle_ref[x1, 1:2, :]
@@ -195,37 +221,30 @@
             ]
 
 
-def correct_kernel(index_ref, plane_ref, data_ref, real_ref, imaginary_ref):
-    rows = real_ref.shape[0]
-    x = lax.broadcasted_iota(jnp.int32, (rows, TILE), 0) + index_ref[0] * rows
-    y = lax.broadcasted_iota(jnp.int32, (rows, TILE), 1) + index_ref[1] * TILE
-    along_l = (x - NU // 2).astype(f32) * (1.0 / NU)
-    along_m = (y - NV // 2).astype(f32) * (1.0 / NV)
-    height = jnp.sqrt(1.0 - along_l * along_l - along_m * along_m)
-    phase = 2.0 * math.pi * plane_ref[0] * (height - 1.0)
+def phase_factors(plane, x, y):
+    along_l = (x - NU // 2).astype(f32) / NU
+    along_m = (y - NV // 2).astype(f32) / NV
+    height = jnp.sqrt(
+        1.0 - along_l[:, None] * along_l[:, None] - along_m[None, :] * along_m[None, :]
+    )
+    phase = 2.0 * math.pi * plane * (height - 1.0)
     scale = 1.0 / math.sqrt(NU * NV)
-    cosine = jnp.cos(phase) * scale
-    sine = jnp.sin(phase) * scale
-    a = data_ref[:, :8, :].reshape(rows, TILE)
-    b = data_ref[:, 8:, :].reshape(rows, TILE)
-    real_ref[...] = a * cosine - b * sine
-    imaginary_ref[...] = a * sine + b * cosine
+    return lax.optimization_barrier((jnp.cos(phase) * scale, jnp.sin(phase) * scale))
 
 
 VMEM = pl.BlockSpec(memory_space=pltpu.VMEM)
 SMEM = pl.BlockSpec(memory_space=pltpu.SMEM)
-
-
-def call(kernel, outs, in_specs, scratch=(), grid=()):
-    single = not isinstance(outs, list)
+HBM = pl.BlockSpec(memory_space=pltpu.HBM)
+
+
+def call(kernel, outs, in_specs, scratch=(), vmem=32):
     return pl.pallas_call(
         kernel,
         out_shape=outs,
-        grid=grid,
         in_specs=in_specs,
-        out_specs=VMEM if single else [VMEM] * len(outs),
+        out_specs=VMEM,
         scratch_shapes=list(scratch),
-        compiler_params=pltpu.CompilerParams(vmem_limit_bytes=32 * 1024 * 1024),
+        compiler_params=pltpu.CompilerParams(vmem_limit_bytes=vmem * 1024 * 1024),
     )
 
 
@@ -234,20 +253,30 @@
         return jax.ShapeDtypeStruct(dims, f32)
 
     length = 2 * PART * SLOTS + SLOTS
-    pieces = call(grid_kernel, shape(GROUPS, length, TILE), [SMEM, SMEM, VMEM, VMEM])(
-        counts, tile_row, visibilities, coords
+    pieces = call(
+        grid_kernel,
+        shape(GROUPS, length, TILE),
+        [SMEM, HBM, HBM, HBM],
+        [
+            pltpu.SMEM((1, SLOTS), jnp.int32),
+            pltpu.VMEM((SLOTS, 2, BLOCK), f32),
+            pltpu.VMEM((SLOTS, 2, BLOCK), f32),
+            pltpu.SemaphoreType.DMA(()),
+            pltpu.SemaphoreType.DMA((2, SLOTS)),
+        ],
+    )(
+        counts,
+        pltpu.with_memory_space_constraint(tile_row.reshape(1, SLOTS), pltpu.HBM),
+        pltpu.with_memory_space_constraint(visibilities, pltpu.HBM),
+        pltpu.with_memory_space_constraint(coords, pltpu.HBM),
     )
     pieces = lax.all_to_all(pieces, "tm", 0, 0, tiled=True)
-    label_spec = pl.BlockSpec(
-        (GROUPS, SLOTS, TILE), lambda step: (0, 2 * PART, 0), memory_space=pltpu.SMEM
-    )
     spectrum = call(
         transform_u_kernel,
         shape(512, TILE),
-        [label_spec, VMEM, VMEM, VMEM],
-        [pltpu.VMEM((TROWS + 1, 2 * PART, TILE), f32), pltpu.VMEM((256, 256), f32)],
-        (1,),
-    )(pieces, pieces, jnp.asarray(inner_u_table()), jnp.asarray(twiddle_u_table()))
+        [VMEM, VMEM, VMEM],
+        [pltpu.VMEM((2, TROWS + 1, 2 * PART, TILE), f32), pltpu.VMEM((256, 256), f32)],
+    )(pieces, jnp.asarray(inner_u_table()), jnp.asarray(twiddle_u_table()))
     spectrum = lax.all_to_all(
         spectrum.reshape(256, 2, TILE), ("tm", "col"), 0, 0, tiled=True
     ).reshape(512, TILE)
@@ -263,11 +292,13 @@
         jnp.asarray(inner_v_table()),
     )
     image = lax.all_to_all(image, "col", 0, 0, tiled=True)
-    index = jnp.stack([lax.axis_index("tm"), lax.axis_index("col")]).astype(jnp.int32)
     rows = NU // GROUPS
-    return tuple(
-        call(correct_kernel, [shape(rows, TILE)] * 2, [SMEM, SMEM, VMEM])(index, w_plane, image)
-    )
+    x = lax.axis_index("tm") * rows + jnp.arange(rows, dtype=jnp.int32)
+    y = lax.axis_index("col") * TILE + jnp.arange(TILE, dtype=jnp.int32)
+    cosine, sine = phase_factors(w_plane[0], x, y)
+    real = image[:, :8, :].reshape(rows, TILE)
+    imaginary = image[:, 8:, :].reshape(rows, TILE)
+    return real * cosine - imaginary * sine, real * sine + imaginary * cosine
 
 
 def solution(mesh):

time: 79.6 us -> 75.1 us (0.943)
  Pallas kernels: 6.94 us -> 3.65 us
  local copies, waits for them, and re-layouts: 2.56 us -> 0.03 us
  other arithmetic: 0.08 us -> 1.33 us
    pallas_call x3 -> x2, Pallas kernels: 5.63 us -> 2.35 us  [the longest x1 1.61 us: shards(): call(grid_kernel, shape(GROUPS, length, TILE), [SMEM, HBM, HBM, HBM], [pl...]
    all_to_all x1, blocking collectives: 19.9 us -> 23 us  [shards(): pieces = lax.all_to_all(pieces, 'tm', 0, 0, tiled=True)]
    all_to_all x1, blocking collectives: 31.3 us -> 28.7 us  [shards(): lax.all_to_all(spectrum.reshape(256, 2, TILE), ('tm', 'col'), 0, 0, tiled...]
    unnamed x15 -> x10, local copies, waits for them, and re-layouts: 2.56 us -> 0.03 us
  transfers between devices with their start and end apart: 1 -> 1, of which waited for: 1 -> 1; matrix products, arithmetic and copies ran while one was open for 0% -> 1% of each run, Pallas kernels for 0% -> 0%
where the time goes in v2:
time: 75.1 us; the launch traced here: 75 us
  blocking collectives  51.7 us (69%)
  waiting for transfers between devices  12.3 us (16%)
  starting transfers between devices  3.98 us (5%)
  Pallas kernels  3.65 us (5%)
  between operations  2.01 us (3%)
  other arithmetic  1.33 us (2%)
    all_to_all x1, blocking collectives, shards(): lax.all_to_all(spectrum.reshape(256, 2, TILE), ('tm', 'col'), 0, 0, tiled...  28.7 us
    all_to_all x1, blocking collectives, shards(): pieces = lax.all_to_all(pieces, 'tm', 0, 0, tiled=True)  23 us
    all_to_all x1, waiting for transfers between devices, shards(): image = lax.all_to_all(image, 'col', 0, 0, tiled=True)  12.3 us
    all_to_all x1, starting transfers between devices, shards(): image = lax.all_to_all(image, 'col', 0, 0, tiled=True)  3.98 us
    pallas_call x1, Pallas kernels, shards(): call(grid_kernel, shape(GROUPS, length, TILE), [SMEM, HBM, HBM, HBM], [pl...  1.61 us
  transfers between devices with their start and end apart: 1, of which 1 were waited for; matrix products, arithmetic and copies ran while one was open for 1% of the time, Pallas kernels for 0%

profile of v2, /device:TPU:1, one launch (start us, length us, event | category | flops | bytes accessed | tf_op | source)
XLA Modules:
  0.0 75.0 jit_solution(5543034029789733022)
XLA Ops:
  1.3 1.6 %shard_map.113 = f32[8,264,128]{2,1,0:T(8,128)S(1)} custom-call(s32[1,1]{1,0:T(1,128)S(6)} %copy.12.count_ref, s32[1,8]{1,0:T(1,128)} %bitcast.18, f32[8,1,2,2048]{3,2,1,0:T(2,128)} %vis_hbm.1, f32[8,1,2,2048]{3,2,1,0:T(2,128)} %place_hbm.1), custom_call_target="tpu_custom_call" | custom-call | tf_op jit(solution)/shard_map/pallas_call | solution.py:256
  2.9 0.0 copy-start.3
  2.9 0.0 copy-start.4
  2.9 23.0 %all_to_all.15.piece_ref = f32[8,264,128]{2,1,0:T(8,128)S(1)} all-to-all(f32[8,264,128]{2,1,0:T(8,128)S(1)} %shard_map.113), channel_id=1, replica_groups=mesh['tm'=8,'col'=32] {'tm'}, dimensions={0} | all-to-all | bytes 2162688 | tf_op jit(solution)/shard_map/all_to_all | solution.py:273
  25.9 0.0 copy-done.3
  25.9 0.0 copy-done.4
  25.9 0.0 copy-start
  25.9 0.0 copy-start.1
  25.9 0.0 copy-start.2
  25.9 0.7 shard_map.114
  26.7 28.7 %all_to_all.16 = f32[256,2,128]{2,1,0:T(2,128)S(1)} all-to-all(f32[256,2,128]{2,1,0:T(2,128)S(1)} %bitcast.17), channel_id=1, replica_groups=mesh['tm'=8,'col'=32] {'tm','col'}, dimensions={0} | all-to-all | bytes 524288 | tf_op jit(solution)/shard_map/all_to_all | solution.py:280
  55.4 0.0 copy-done
  55.4 0.0 copy-done.1
  55.4 0.0 copy-done.2
  55.4 1.3 %shard_map.115 = f32[32,16,128]{2,1,0:T(8,128)} custom-call(f32[512,128]{1,0:T(8,128)S(1)} %bitcast.16, bf16[2,8,64,64]{3,2,1,0:T(8,128)(2,1)S(1)} %copy-done.2, f32[8,2,32,128]{3,2,1,0:T(8,128)S(1)} %copy-done.1, bf16[2,256,256]{2,1,0:T(8,128)(2,1)S(1)} %copy-done), custom_call_target="tpu_custom_call" | custom-call | tf_op jit(solution)/shard_map/pallas_call | solution.py:283
  56.7 4.0 %all-to-all-start.2 = ((f32[32,16,128]{2,1,0:T(8,128)}), f32[32,16,128]{2,1,0:T(8,128)S(1)}, u32[]{:S(2)}, u32[]{:S(2)}) async-start(f32[32,16,128]{2,1,0:T(8,128)} %shard_map.115), calls=%async_computation.2 | async-start | bytes 524288 | tf_op jit(solution)/shard_map/all_to_all | solution.py:294
  61.4 0.6 sine_multiply_fusion
  62.0 12.3 %all-to-all-done.2 = f32[32,16,128]{2,1,0:T(8,128)S(1)} async-done(((f32[32,16,128]{2,1,0:T(8,128)}), f32[32,16,128]{2,1,0:T(8,128)S(1)}, u32[]{:S(2)}, u32[]{:S(2)}) %all-to-all-start.2) | async-done | bytes 262176 | tf_op jit(solution)/shard_map/all_to_all | solution.py:294
  74.3 0.7 multiply_add_fusion
  (2 shorter events, 0.0 us)
Async XLA Ops:
  2.9 23.0 %copy-start.3 = (bf16[2,256,256]{2,1,0:T(8,128)(2,1)S(1)}, bf16[2,256,256]{2,1,0:T(8,128)(2,1)}, u32[]{:S(2)}) copy-start(bf16[2,256,256]{2,1,0:T(8,128)(2,1)} %constant.45.clone.table_ref) | copy-start | bytes 786436
  2.9 23.0 %copy-start.4 = (f32[16,2,128]{2,1,0:T(2,128)S(1)}, f32[16,2,128]{2,1,0:T(2,128)}, u32[]{:S(2)}) copy-start(f32[16,2,128]{2,1,0:T(2,128)} %constant.46.clone.twiddle_ref) | copy-start | bytes 49156
  25.9 29.5 %copy-start = (bf16[2,256,256]{2,1,0:T(8,128)(2,1)S(1)}, bf16[2,256,256]{2,1,0:T(8,128)(2,1)}, u32[]{:S(2)}) copy-start(bf16[2,256,256]{2,1,0:T(8,128)(2,1)} %constant.49.clone.table_ref) | copy-start | bytes 786436
  25.9 29.5 %copy-start.1 = (f32[8,2,32,128]{3,2,1,0:T(8,128)S(1)}, f32[8,2,32,128]{3,2,1,0:T(8,128)}, u32[]{:S(2)}) copy-start(f32[8,2,32,128]{3,2,1,0:T(8,128)} %constant.48.clone.twiddle_ref) | copy-start | bytes 786436
  25.9 29.5 %copy-start.2 = (bf16[2,8,64,64]{3,2,1,0:T(8,128)(2,1)S(1)}, bf16[2,8,64,64]{3,2,1,0:T(8,128)(2,1)}, u32[]{:S(2)}) copy-start(bf16[2,8,64,64]{3,2,1,0:T(8,128)(2,1)} %constant.47.clone.column_ref) | copy-start | bytes 393220
  56.7 17.6 %all-to-all-start.2 = ((f32[32,16,128]{2,1,0:T(8,128)}), f32[32,16,128]{2,1,0:T(8,128)S(1)}, u32[]{:S(2)}, u32[]{:S(2)}) async-start(f32[32,16,128]{2,1,0:T(8,128)} %shard_map.115), calls=%async_computation.2 | async-start | bytes 524288 | tf_op jit(solution)/shard_map/all_to_all | solution.py:294

commit v3 on v2

--- a/solution.py
+++ b/solution.py
@@ -144,14 +144,9 @@
 
     rows.wait()
     count = count_ref[0, 0]
-    slot_of = lax.broadcasted_iota(jnp.int32, (SLOTS, TILE), 0)
-    label = jnp.full((SLOTS, TILE), TROWS, jnp.int32)
     for slot in range(SLOTS):
-        here = jnp.where(slot < count, row_ref[0, slot], TROWS)
-        label = jnp.where(slot_of == slot, here, label)
-    label = label.astype(f32)
-    for g in range(GROUPS):
-        out_ref[g, 2 * PART * SLOTS :, :] = label
+        row = jnp.where(slot < count, row_ref[0, slot], TROWS).astype(f32)
+        out_ref[:, 2 * PART * slot : 2 * PART * slot + 8, :] = jnp.full((GROUPS, 8, TILE), row)
 
     cells = lax.broadcasted_iota(jnp.int32, (TILE, CHUNK), 0).astype(f32)
 
@@ -159,6 +154,8 @@
         offset = cells - position
         inside = jnp.maximum(1.0 - offset * offset, 0.0)
         return (inside * inside).astype(bf16)
+
+    corner = lax.broadcasted_iota(jnp.int32, (GROUPS, PART, TILE), 2) == 0
 
     def one_slot(slot, carry):
         wait(slot, 0)
@@ -173,6 +170,8 @@
             total += lax.dot_general(weight_v, weighted, NT, preferred_element_type=f32)
         for part in range(2):
             piece = total[:, part * TILE : (part + 1) * TILE].reshape(GROUPS, PART, TILE)
+            if part == 0:
+                piece = jnp.where(corner, row_ref[0, slot].astype(f32), piece)
             first = pl.multiple_of(slot * (2 * PART) + part * PART, PART)
             out_ref[:, pl.ds(first, PART), :] = piece
         return carry
@@ -184,12 +183,13 @@
 def transform_u_kernel(piece_ref, table_ref, twiddle_ref, out_ref, grid_ref, rows_ref):
     grid_ref[...] = jnp.zeros_like(grid_ref)
     for t in range(GROUPS):
-        label = piece_ref[t, 2 * PART * SLOTS :, :].astype(jnp.int32)
         for slot in range(SLOTS):
-            row = label[slot, 0]
-            grid_ref[slot % 2, row] += piece_ref[t, 2 * PART * slot : 2 * PART * (slot + 1), :]
+            piece = piece_ref[t, 2 * PART * slot : 2 * PART * (slot + 1), :]
+            row = piece[0, 0].astype(jnp.int32)
+            grid_ref[slot % 2, row] += piece
     cells = [grid_ref[0, r] + grid_ref[1, r] for r in range(TROWS)]
-    items = [(cell[:PART], cell[PART:]) for cell in cells]
+    reached = lax.broadcasted_iota(jnp.int32, (PART, TILE), 1) > 0
+    items = [(jnp.where(reached, cell[:PART], 0.0), cell[PART:]) for cell in cells]
     for x1, (a, b) in enumerate(fft(items)):
         c = twiddle_ref[x1, 0:1, :]
         s = twiddle_ref[x1, 1:2, :]
@@ -252,7 +252,7 @@
     def shape(*dims):
         return jax.ShapeDtypeStruct(dims, f32)
 
-    length = 2 * PART * SLOTS + SLOTS
+    length = 2 * PART * SLOTS
     pieces = call(
         grid_kernel,
         shape(GROUPS, length, TILE),

time: 75.1 us -> 74.4 us (level)
  blocking collectives: 51.7 us -> 50.5 us
    all_to_all x1, blocking collectives: 23 us -> 21.3 us  [shards(): pieces = lax.all_to_all(pieces, 'tm', 0, 0, tiled=True)]
where the time goes in v3:
time: 74.4 us; the launch traced here: 74.5 us
  blocking collectives  50.5 us (68%)
  waiting for transfers between devices  12.3 us (17%)
  Pallas kernels  4.29 us (6%)
  starting transfers between devices  3.99 us (5%)
  between operations  2.01 us (3%)
  other arithmetic  1.33 us (2%)
    all_to_all x1, blocking collectives, shards(): lax.all_to_all(spectrum.reshape(256, 2, TILE), ('tm', 'col'), 0, 0, tiled...  29.3 us
    all_to_all x1, blocking collectives, shards(): pieces = lax.all_to_all(pieces, 'tm', 0, 0, tiled=True)  21.3 us
    all_to_all x1, waiting for transfers between devices, shards(): image = lax.all_to_all(image, 'col', 0, 0, tiled=True)  12.3 us
    all_to_all x1, starting transfers between devices, shards(): image = lax.all_to_all(image, 'col', 0, 0, tiled=True)  3.99 us
    pallas_call x1, Pallas kernels, shards(): call(grid_kernel, shape(GROUPS, length, TILE), [SMEM, HBM, HBM, HBM], [pl...  2.21 us
  transfers between devices with their start and end apart: 1, of which 1 were waited for; matrix products, arithmetic and copies ran while one was open for 1% of the time, Pallas kernels for 0%

profile of v3, /device:TPU:1, one launch (start us, length us, event | category | flops | bytes accessed | tf_op | source)
XLA Modules:
  0.0 74.5 jit_solution(11826511547737862259)
XLA Ops:
  1.3 2.2 %shard_map.113 = f32[8,256,128]{2,1,0:T(8,128)S(1)} custom-call(s32[1,1]{1,0:T(1,128)S(6)} %copy.12.count_ref, s32[1,8]{1,0:T(1,128)} %bitcast.18, f32[8,1,2,2048]{3,2,1,0:T(2,128)} %vis_hbm.1, f32[8,1,2,2048]{3,2,1,0:T(2,128)} %place_hbm.1), custom_call_target="tpu_custom_call" | custom-call | tf_op jit(solution)/shard_map/pallas_call | solution.py:256
  3.5 0.0 copy-start.3
  3.5 0.0 copy-start.4
  3.5 21.3 %all_to_all.15.piece_ref = f32[8,256,128]{2,1,0:T(8,128)S(1)} all-to-all(f32[8,256,128]{2,1,0:T(8,128)S(1)} %shard_map.113), channel_id=1, replica_groups=mesh['tm'=8,'col'=32] {'tm'}, dimensions={0} | all-to-all | bytes 2097152 | tf_op jit(solution)/shard_map/all_to_all | solution.py:273
  24.8 0.0 copy-done.3
  24.8 0.0 copy-done.4
  24.8 0.0 copy-start.2
  24.8 0.8 %shard_map.114 = f32[512,128]{1,0:T(8,128)S(1)} custom-call(f32[8,256,128]{2,1,0:T(8,128)S(1)} %all_to_all.15.piece_ref, bf16[2,256,256]{2,1,0:T(8,128)(2,1)S(1)} %copy-done.3, f32[16,2,128]{2,1,0:T(2,128)S(1)} %copy-done.4), custom_call_target="tpu_custom_call" | custom-call | tf_op jit(solution)/shard_map/pallas_call | solution.py:274
  25.6 0.0 copy-start
  25.6 0.0 copy-start.1
  25.6 29.3 %all_to_all.16 = f32[256,2,128]{2,1,0:T(2,128)S(1)} all-to-all(f32[256,2,128]{2,1,0:T(2,128)S(1)} %bitcast.17), channel_id=1, replica_groups=mesh['tm'=8,'col'=32] {'tm','col'}, dimensions={0} | all-to-all | bytes 524288 | tf_op jit(solution)/shard_map/all_to_all | solution.py:280
  54.9 0.0 copy-done.2
  54.9 0.0 copy-done
  54.9 0.0 copy-done.1
  54.9 1.3 %shard_map.115 = f32[32,16,128]{2,1,0:T(8,128)} custom-call(f32[512,128]{1,0:T(8,128)S(1)} %bitcast.16, bf16[2,8,64,64]{3,2,1,0:T(8,128)(2,1)S(1)} %copy-done.2, f32[8,2,32,128]{3,2,1,0:T(8,128)S(1)} %copy-done.1, bf16[2,256,256]{2,1,0:T(8,128)(2,1)S(1)} %copy-done), custom_call_target="tpu_custom_call" | custom-call | tf_op jit(solution)/shard_map/pallas_call | solution.py:283
  56.2 4.0 %all-to-all-start.2 = ((f32[32,16,128]{2,1,0:T(8,128)}), f32[32,16,128]{2,1,0:T(8,128)S(1)}, u32[]{:S(2)}, u32[]{:S(2)}) async-start(f32[32,16,128]{2,1,0:T(8,128)} %shard_map.115), calls=%async_computation.2 | async-start | bytes 524288 | tf_op jit(solution)/shard_map/all_to_all | solution.py:294
  60.9 0.6 sine_multiply_fusion
  61.4 12.3 %all-to-all-done.2 = f32[32,16,128]{2,1,0:T(8,128)S(1)} async-done(((f32[32,16,128]{2,1,0:T(8,128)}), f32[32,16,128]{2,1,0:T(8,128)S(1)}, u32[]{:S(2)}, u32[]{:S(2)}) %all-to-all-start.2) | async-done | bytes 262176 | tf_op jit(solution)/shard_map/all_to_all | solution.py:294
  73.7 0.7 multiply_add_fusion
  (2 shorter events, 0.0 us)
Async XLA Ops:
  3.5 21.3 %copy-start.3 = (bf16[2,256,256]{2,1,0:T(8,128)(2,1)S(1)}, bf16[2,256,256]{2,1,0:T(8,128)(2,1)}, u32[]{:S(2)}) copy-start(bf16[2,256,256]{2,1,0:T(8,128)(2,1)} %constant.45.clone.table_ref) | copy-start | bytes 786436
  3.5 21.3 %copy-start.4 = (f32[16,2,128]{2,1,0:T(2,128)S(1)}, f32[16,2,128]{2,1,0:T(2,128)}, u32[]{:S(2)}) copy-start(f32[16,2,128]{2,1,0:T(2,128)} %constant.46.clone.twiddle_ref) | copy-start | bytes 49156
  24.8 30.1 %copy-start.2 = (bf16[2,8,64,64]{3,2,1,0:T(8,128)(2,1)S(1)}, bf16[2,8,64,64]{3,2,1,0:T(8,128)(2,1)}, u32[]{:S(2)}) copy-start(bf16[2,8,64,64]{3,2,1,0:T(8,128)(2,1)} %constant.47.clone.column_ref) | copy-start | bytes 393220
  25.6 29.3 %copy-start = (bf16[2,256,256]{2,1,0:T(8,128)(2,1)S(1)}, bf16[2,256,256]{2,1,0:T(8,128)(2,1)}, u32[]{:S(2)}) copy-start(bf16[2,256,256]{2,1,0:T(8,128)(2,1)} %constant.49.clone.table_ref) | copy-start | bytes 786436
  25.6 29.3 %copy-start.1 = (f32[8,2,32,128]{3,2,1,0:T(8,128)S(1)}, f32[8,2,32,128]{3,2,1,0:T(8,128)}, u32[]{:S(2)}) copy-start(f32[8,2,32,128]{3,2,1,0:T(8,128)} %constant.48.clone.twiddle_ref) | copy-start | bytes 786436
  56.2 17.6 %all-to-all-start.2 = ((f32[32,16,128]{2,1,0:T(8,128)}), f32[32,16,128]{2,1,0:T(8,128)S(1)}, u32[]{:S(2)}, u32[]{:S(2)}) async-start(f32[32,16,128]{2,1,0:T(8,128)} %shard_map.115), calls=%async_computation.2 | async-start | bytes 524288 | tf_op jit(solution)/shard_map/all_to_all | solution.py:294

commit v4 on v3

--- a/solution.py
+++ b/solution.py
@@ -148,12 +148,23 @@
         row = jnp.where(slot < count, row_ref[0, slot], TROWS).astype(f32)
         out_ref[:, 2 * PART * slot : 2 * PART * slot + 8, :] = jnp.full((GROUPS, 8, TILE), row)
 
-    cells = lax.broadcasted_iota(jnp.int32, (TILE, CHUNK), 0).astype(f32)
-
-    def taper(position):
-        offset = cells - position
+    cells = lax.broadcasted_iota(jnp.int32, (TILE, CHUNK), 0).astype(f32).astype(bf16)
+    none = jnp.zeros((TILE, CHUNK), bf16)
+
+    def taper(offset):
         inside = jnp.maximum(1.0 - offset * offset, 0.0)
         return (inside * inside).astype(bf16)
+
+    def reached(position):
+        first = jnp.floor(position)
+        second = first + 1.0
+        return (
+            (cells == first.astype(bf16), taper(first - position)),
+            (cells == second.astype(bf16), taper(second - position)),
+        )
+
+    def spread(places, values):
+        return jnp.where(places[0], values[0], jnp.where(places[1], values[1], none))
 
     corner = lax.broadcasted_iota(jnp.int32, (GROUPS, PART, TILE), 2) == 0
 
@@ -162,10 +173,17 @@
         total = jnp.zeros((TILE, 2 * TILE), f32)
         for start in range(0, BLOCK, CHUNK):
             at = pl.ds(start, CHUNK)
-            weight_u = taper(place_ref[slot, 0:1, at])
-            weight_v = taper(place_ref[slot, 1:2, at])
-            real = weight_u * vis_ref[slot, 0:1, at].astype(bf16)
-            imaginary = weight_u * vis_ref[slot, 1:2, at].astype(bf16)
+            (here_u, first_u), (next_u, second_u) = reached(place_ref[slot, 0:1, at])
+            (here_v, first_v), (next_v, second_v) = reached(place_ref[slot, 1:2, at])
+            weight_v = spread((here_v, next_v), (first_v, second_v))
+            first_u, second_u = first_u.astype(f32), second_u.astype(f32)
+            real, imaginary = (
+                spread(
+                    (here_u, next_u),
+                    ((first_u * value).astype(bf16), (second_u * value).astype(bf16)),
+                )
+                for value in (vis_ref[slot, 0:1, at], vis_ref[slot, 1:2, at])
+            )
             weighted = jnp.concatenate([real, imaginary], 0)
             total += lax.dot_general(weight_v, weighted, NT, preferred_element_type=f32)
         for part in range(2):

time: 74.4 us -> 74.2 us (level)
    all_to_all x1, blocking collectives: 29.3 us -> 28.5 us  [shards(): lax.all_to_all(spectrum.reshape(256, 2, TILE), ('tm', 'col'), 0, 0, tiled...]
where the time goes in v4:
time: 74.2 us; the launch traced here: 74.3 us
  blocking collectives  50 us (67%)
  waiting for transfers between devices  12.3 us (17%)
  Pallas kernels  4.62 us (6%)
  starting transfers between devices  3.99 us (5%)
  between operations  2.01 us (3%)
  other arithmetic  1.33 us (2%)
    all_to_all x1, blocking collectives, shards(): lax.all_to_all(spectrum.reshape(256, 2, TILE), ('tm', 'col'), 0, 0, tiled...  28.5 us
    all_to_all x1, blocking collectives, shards(): pieces = lax.all_to_all(pieces, 'tm', 0, 0, tiled=True)  21.5 us
    all_to_all x1, waiting for transfers between devices, shards(): image = lax.all_to_all(image, 'col', 0, 0, tiled=True)  12.3 us
    all_to_all x1, starting transfers between devices, shards(): image = lax.all_to_all(image, 'col', 0, 0, tiled=True)  3.99 us
    pallas_call x1, Pallas kernels, shards(): call(grid_kernel, shape(GROUPS, length, TILE), [SMEM, HBM, HBM, HBM], [pl...  2.54 us
  transfers between devices with their start and end apart: 1, of which 1 were waited for; matrix products, arithmetic and copies ran while one was open for 1% of the time, Pallas kernels for 0%

profile of v4, /device:TPU:1, one launch (start us, length us, event | category | flops | bytes accessed | tf_op | source)
XLA Modules:
  0.0 74.3 jit_solution(13299135981168632793)
XLA Ops:
  1.3 2.5 %shard_map.113 = f32[8,256,128]{2,1,0:T(8,128)S(1)} custom-call(s32[1,1]{1,0:T(1,128)S(6)} %copy.12.count_ref, s32[1,8]{1,0:T(1,128)} %bitcast.18, f32[8,1,2,2048]{3,2,1,0:T(2,128)} %vis_hbm.1, f32[8,1,2,2048]{3,2,1,0:T(2,128)} %place_hbm.1), custom_call_target="tpu_custom_call" | custom-call | tf_op jit(solution)/shard_map/pallas_call | solution.py:274
  3.8 0.0 copy-start.3
  3.8 0.0 copy-start.4
  3.9 21.5 %all_to_all.15.piece_ref = f32[8,256,128]{2,1,0:T(8,128)S(1)} all-to-all(f32[8,256,128]{2,1,0:T(8,128)S(1)} %shard_map.113), channel_id=1, replica_groups=mesh['tm'=8,'col'=32] {'tm'}, dimensions={0} | all-to-all | bytes 2097152 | tf_op jit(solution)/shard_map/all_to_all | solution.py:291
  25.4 0.0 copy-done.3
  25.4 0.0 copy-done.4
  25.4 0.0 copy-start.2
  25.4 0.8 %shard_map.114 = f32[512,128]{1,0:T(8,128)S(1)} custom-call(f32[8,256,128]{2,1,0:T(8,128)S(1)} %all_to_all.15.piece_ref, bf16[2,256,256]{2,1,0:T(8,128)(2,1)S(1)} %copy-done.3, f32[16,2,128]{2,1,0:T(2,128)S(1)} %copy-done.4), custom_call_target="tpu_custom_call" | custom-call | tf_op jit(solution)/shard_map/pallas_call | solution.py:292
  26.2 0.0 copy-start
  26.2 0.0 copy-start.1
  26.2 28.5 %all_to_all.16 = f32[256,2,128]{2,1,0:T(2,128)S(1)} all-to-all(f32[256,2,128]{2,1,0:T(2,128)S(1)} %bitcast.17), channel_id=1, replica_groups=mesh['tm'=8,'col'=32] {'tm','col'}, dimensions={0} | all-to-all | bytes 524288 | tf_op jit(solution)/shard_map/all_to_all | solution.py:298
  54.7 0.0 copy-done.2
  54.7 0.0 copy-done
  54.7 0.0 copy-done.1
  54.7 1.3 %shard_map.115 = f32[32,16,128]{2,1,0:T(8,128)} custom-call(f32[512,128]{1,0:T(8,128)S(1)} %bitcast.16, bf16[2,8,64,64]{3,2,1,0:T(8,128)(2,1)S(1)} %copy-done.2, f32[8,2,32,128]{3,2,1,0:T(8,128)S(1)} %copy-done.1, bf16[2,256,256]{2,1,0:T(8,128)(2,1)S(1)} %copy-done), custom_call_target="tpu_custom_call" | custom-call | tf_op jit(solution)/shard_map/pallas_call | solution.py:301
  56.0 4.0 %all-to-all-start.2 = ((f32[32,16,128]{2,1,0:T(8,128)}), f32[32,16,128]{2,1,0:T(8,128)S(1)}, u32[]{:S(2)}, u32[]{:S(2)}) async-start(f32[32,16,128]{2,1,0:T(8,128)} %shard_map.115), calls=%async_computation.2 | async-start | bytes 524288 | tf_op jit(solution)/shard_map/all_to_all | solution.py:312
  60.7 0.6 sine_multiply_fusion
  61.2 12.3 %all-to-all-done.2 = f32[32,16,128]{2,1,0:T(8,128)S(1)} async-done(((f32[32,16,128]{2,1,0:T(8,128)}), f32[32,16,128]{2,1,0:T(8,128)S(1)}, u32[]{:S(2)}, u32[]{:S(2)}) %all-to-all-start.2) | async-done | bytes 262176 | tf_op jit(solution)/shard_map/all_to_all | solution.py:312
  73.5 0.7 multiply_add_fusion
  (2 shorter events, 0.0 us)
Async XLA Ops:
  3.8 21.6 %copy-start.3 = (bf16[2,256,256]{2,1,0:T(8,128)(2,1)S(1)}, bf16[2,256,256]{2,1,0:T(8,128)(2,1)}, u32[]{:S(2)}) copy-start(bf16[2,256,256]{2,1,0:T(8,128)(2,1)} %constant.45.clone.table_ref) | copy-start | bytes 786436
  3.8 21.6 %copy-start.4 = (f32[16,2,128]{2,1,0:T(2,128)S(1)}, f32[16,2,128]{2,1,0:T(2,128)}, u32[]{:S(2)}) copy-start(f32[16,2,128]{2,1,0:T(2,128)} %constant.46.clone.twiddle_ref) | copy-start | bytes 49156
  25.4 29.3 %copy-start.2 = (bf16[2,8,64,64]{3,2,1,0:T(8,128)(2,1)S(1)}, bf16[2,8,64,64]{3,2,1,0:T(8,128)(2,1)}, u32[]{:S(2)}) copy-start(bf16[2,8,64,64]{3,2,1,0:T(8,128)(2,1)} %constant.47.clone.column_ref) | copy-start | bytes 393220
  26.2 28.5 %copy-start = (bf16[2,256,256]{2,1,0:T(8,128)(2,1)S(1)}, bf16[2,256,256]{2,1,0:T(8,128)(2,1)}, u32[]{:S(2)}) copy-start(bf16[2,256,256]{2,1,0:T(8,128)(2,1)} %constant.49.clone.table_ref) | copy-start | bytes 786436
  26.2 28.5 %copy-start.1 = (f32[8,2,32,128]{3,2,1,0:T(8,128)S(1)}, f32[8,2,32,128]{3,2,1,0:T(8,128)}, u32[]{:S(2)}) copy-start(f32[8,2,32,128]{3,2,1,0:T(8,128)} %constant.48.clone.twiddle_ref) | copy-start | bytes 786436
  56.0 17.6 %all-to-all-start.2 = ((f32[32,16,128]{2,1,0:T(8,128)}), f32[32,16,128]{2,1,0:T(8,128)S(1)}, u32[]{:S(2)}, u32[]{:S(2)}) async-start(f32[32,16,128]{2,1,0:T(8,128)} %shard_map.115), calls=%async_computation.2 | async-start | bytes 524288 | tf_op jit(solution)/shard_map/all_to_all | solution.py:312

commit v5 on v4

--- a/solution.py
+++ b/solution.py
@@ -127,20 +127,12 @@
     rows = pltpu.make_async_copy(row_hbm, row_ref, known)
     rows.start()
 
-    def fetch(slot):
-        return (
-            pltpu.make_async_copy(vis_hbm.at[slot, 0], vis_ref.at[slot], arrived.at[0, slot]),
-            pltpu.make_async_copy(place_hbm.at[slot, 0], place_ref.at[slot], arrived.at[1, slot]),
-        )
-
-    for slot in range(SLOTS):
-        for copy in fetch(slot):
-            copy.start()
-
-    def wait(slot, carry):
-        for copy in fetch(slot):
-            copy.wait()
-        return carry
+    fetches = (
+        pltpu.make_async_copy(place_hbm, place_ref, arrived.at[0]),
+        pltpu.make_async_copy(vis_hbm, vis_ref, arrived.at[1]),
+    )
+    for copy in fetches:
+        copy.start()
 
     rows.wait()
     count = count_ref[0, 0]
@@ -169,12 +161,11 @@
     corner = lax.broadcasted_iota(jnp.int32, (GROUPS, PART, TILE), 2) == 0
 
     def one_slot(slot, carry):
-        wait(slot, 0)
         total = jnp.zeros((TILE, 2 * TILE), f32)
         for start in range(0, BLOCK, CHUNK):
             at = pl.ds(start, CHUNK)
-            (here_u, first_u), (next_u, second_u) = reached(place_ref[slot, 0:1, at])
-            (here_v, first_v), (next_v, second_v) = reached(place_ref[slot, 1:2, at])
+            (here_u, first_u), (next_u, second_u) = reached(place_ref[slot, 0, 0:1, at])
+            (here_v, first_v), (next_v, second_v) = reached(place_ref[slot, 0, 1:2, at])
             weight_v = spread((here_v, next_v), (first_v, second_v))
             first_u, second_u = first_u.astype(f32), second_u.astype(f32)
             real, imaginary = (
@@ -182,7 +173,7 @@
                     (here_u, next_u),
                     ((first_u * value).astype(bf16), (second_u * value).astype(bf16)),
                 )
-                for value in (vis_ref[slot, 0:1, at], vis_ref[slot, 1:2, at])
+                for value in (vis_ref[slot, 0, 0:1, at], vis_ref[slot, 0, 1:2, at])
             )
             weighted = jnp.concatenate([real, imaginary], 0)
             total += lax.dot_general(weight_v, weighted, NT, preferred_element_type=f32)
@@ -194,8 +185,9 @@
             out_ref[:, pl.ds(first, PART), :] = piece
         return carry
 
+    for copy in fetches:
+        copy.wait()
     lax.fori_loop(0, count, one_slot, 0)
-    lax.fori_loop(count, SLOTS, wait, 0)
 
 
 def transform_u_kernel(piece_ref, table_ref, twiddle_ref, out_ref, grid_ref, rows_ref):
@@ -277,10 +269,10 @@
         [SMEM, HBM, HBM, HBM],
         [
             pltpu.SMEM((1, SLOTS), jnp.int32),
-            pltpu.VMEM((SLOTS, 2, BLOCK), f32),
-            pltpu.VMEM((SLOTS, 2, BLOCK), f32),
+            pltpu.VMEM((SLOTS, 1, 2, BLOCK), f32),
+            pltpu.VMEM((SLOTS, 1, 2, BLOCK), f32),
             pltpu.SemaphoreType.DMA(()),
-            pltpu.SemaphoreType.DMA((2, SLOTS)),
+            pltpu.SemaphoreType.DMA((2,)),
         ],
     )(
         counts,

time: 74.2 us -> 74.7 us (level); the launches traced: 74.3 us -> 74 us
  blocking collectives: 50 us -> 49.2 us
where the time goes in v5:
time: 74.7 us; the launch traced here: 74 us
  blocking collectives  49.2 us (66%)
  waiting for transfers between devices  12.3 us (16%)
  Pallas kernels  5.06 us (7%)
  starting transfers between devices  3.99 us (5%)
  between operations  2.01 us (3%)
  other arithmetic  1.33 us (2%)
    all_to_all x1, blocking collectives, shards(): lax.all_to_all(spectrum.reshape(256, 2, TILE), ('tm', 'col'), 0, 0, tiled...  28.1 us
    all_to_all x1, blocking collectives, shards(): pieces = lax.all_to_all(pieces, 'tm', 0, 0, tiled=True)  21.2 us
    all_to_all x1, waiting for transfers between devices, shards(): image = lax.all_to_all(image, 'col', 0, 0, tiled=True)  12.3 us
    all_to_all x1, starting transfers between devices, shards(): image = lax.all_to_all(image, 'col', 0, 0, tiled=True)  3.99 us
    pallas_call x1, Pallas kernels, shards(): call(grid_kernel, shape(GROUPS, length, TILE), [SMEM, HBM, HBM, HBM], [pl...  2.99 us
  transfers between devices with their start and end apart: 1, of which 1 were waited for; matrix products, arithmetic and copies ran while one was open for 1% of the time, Pallas kernels for 0%

profile of v5, /device:TPU:1, one launch (start us, length us, event | category | flops | bytes accessed | tf_op | source)
XLA Modules:
  0.0 74.0 jit_solution(1335395109558174177)
XLA Ops:
  1.3 3.0 %shard_map.113 = f32[8,256,128]{2,1,0:T(8,128)S(1)} custom-call(s32[1,1]{1,0:T(1,128)S(6)} %copy.12.count_ref, s32[1,8]{1,0:T(1,128)} %bitcast.18, f32[8,1,2,2048]{3,2,1,0:T(2,128)} %vis_hbm.1, f32[8,1,2,2048]{3,2,1,0:T(2,128)} %place_hbm.1), custom_call_target="tpu_custom_call" | custom-call | tf_op jit(solution)/shard_map/pallas_call | solution.py:266
  4.3 0.0 copy-start.3
  4.3 0.0 copy-start.4
  4.3 21.2 %all_to_all.15.piece_ref = f32[8,256,128]{2,1,0:T(8,128)S(1)} all-to-all(f32[8,256,128]{2,1,0:T(8,128)S(1)} %shard_map.113), channel_id=1, replica_groups=mesh['tm'=8,'col'=32] {'tm'}, dimensions={0} | all-to-all | bytes 2097152 | tf_op jit(solution)/shard_map/all_to_all | solution.py:283
  25.4 0.0 copy-done.3
  25.5 0.0 copy-done.4
  25.5 0.0 copy-start.2
  25.5 0.8 %shard_map.114 = f32[512,128]{1,0:T(8,128)S(1)} custom-call(f32[8,256,128]{2,1,0:T(8,128)S(1)} %all_to_all.15.piece_ref, bf16[2,256,256]{2,1,0:T(8,128)(2,1)S(1)} %copy-done.3, f32[16,2,128]{2,1,0:T(2,128)S(1)} %copy-done.4), custom_call_target="tpu_custom_call" | custom-call | tf_op jit(solution)/shard_map/pallas_call | solution.py:284
  26.2 0.0 copy-start
  26.3 0.0 copy-start.1
  26.3 28.1 %all_to_all.16 = f32[256,2,128]{2,1,0:T(2,128)S(1)} all-to-all(f32[256,2,128]{2,1,0:T(2,128)S(1)} %bitcast.17), channel_id=1, replica_groups=mesh['tm'=8,'col'=32] {'tm','col'}, dimensions={0} | all-to-all | bytes 524288 | tf_op jit(solution)/shard_map/all_to_all | solution.py:290
  54.4 0.0 copy-done.2
  54.4 0.0 copy-done
  54.4 0.0 copy-done.1
  54.4 1.3 %shard_map.115 = f32[32,16,128]{2,1,0:T(8,128)} custom-call(f32[512,128]{1,0:T(8,128)S(1)} %bitcast.16, bf16[2,8,64,64]{3,2,1,0:T(8,128)(2,1)S(1)} %copy-done.2, f32[8,2,32,128]{3,2,1,0:T(8,128)S(1)} %copy-done.1, bf16[2,256,256]{2,1,0:T(8,128)(2,1)S(1)} %copy-done), custom_call_target="tpu_custom_call" | custom-call | tf_op jit(solution)/shard_map/pallas_call | solution.py:293
  55.7 4.0 %all-to-all-start.2 = ((f32[32,16,128]{2,1,0:T(8,128)}), f32[32,16,128]{2,1,0:T(8,128)S(1)}, u32[]{:S(2)}, u32[]{:S(2)}) async-start(f32[32,16,128]{2,1,0:T(8,128)} %shard_map.115), calls=%async_computation.2 | async-start | bytes 524288 | tf_op jit(solution)/shard_map/all_to_all | solution.py:304
  60.4 0.6 sine_multiply_fusion
  60.9 12.3 %all-to-all-done.2 = f32[32,16,128]{2,1,0:T(8,128)S(1)} async-done(((f32[32,16,128]{2,1,0:T(8,128)}), f32[32,16,128]{2,1,0:T(8,128)S(1)}, u32[]{:S(2)}, u32[]{:S(2)}) %all-to-all-start.2) | async-done | bytes 262176 | tf_op jit(solution)/shard_map/all_to_all | solution.py:304
  73.2 0.7 multiply_add_fusion
  (2 shorter events, 0.0 us)
Async XLA Ops:
  4.3 21.2 %copy-start.3 = (bf16[2,256,256]{2,1,0:T(8,128)(2,1)S(1)}, bf16[2,256,256]{2,1,0:T(8,128)(2,1)}, u32[]{:S(2)}) copy-start(bf16[2,256,256]{2,1,0:T(8,128)(2,1)} %constant.45.clone.table_ref) | copy-start | bytes 786436
  4.3 21.2 %copy-start.4 = (f32[16,2,128]{2,1,0:T(2,128)S(1)}, f32[16,2,128]{2,1,0:T(2,128)}, u32[]{:S(2)}) copy-start(f32[16,2,128]{2,1,0:T(2,128)} %constant.46.clone.twiddle_ref) | copy-start | bytes 49156
  25.5 28.9 %copy-start.2 = (bf16[2,8,64,64]{3,2,1,0:T(8,128)(2,1)S(1)}, bf16[2,8,64,64]{3,2,1,0:T(8,128)(2,1)}, u32[]{:S(2)}) copy-start(bf16[2,8,64,64]{3,2,1,0:T(8,128)(2,1)} %constant.47.clone.column_ref) | copy-start | bytes 393220
  26.2 28.1 %copy-start = (bf16[2,256,256]{2,1,0:T(8,128)(2,1)S(1)}, bf16[2,256,256]{2,1,0:T(8,128)(2,1)}, u32[]{:S(2)}) copy-start(bf16[2,256,256]{2,1,0:T(8,128)(2,1)} %constant.49.clone.table_ref) | copy-start | bytes 786436
  26.3 28.1 %copy-start.1 = (f32[8,2,32,128]{3,2,1,0:T(8,128)S(1)}, f32[8,2,32,128]{3,2,1,0:T(8,128)}, u32[]{:S(2)}) copy-start(f32[8,2,32,128]{3,2,1,0:T(8,128)} %constant.48.clone.twiddle_ref) | copy-start | bytes 786436
  55.7 17.6 %all-to-all-start.2 = ((f32[32,16,128]{2,1,0:T(8,128)}), f32[32,16,128]{2,1,0:T(8,128)S(1)}, u32[]{:S(2)}, u32[]{:S(2)}) async-start(f32[32,16,128]{2,1,0:T(8,128)} %shard_map.115), calls=%async_computation.2 | async-start | bytes 524288 | tf_op jit(solution)/shard_map/all_to_all | solution.py:304
